TPU v7x, 32 devices: a whole 2x2x4 slice. The times are simulated.
32 devices in a mesh: ctx: 8 (over z, core), fsdp: 4 (over y, x).
Axes of the slice: x: 2, y: 2, z: 4, core: 2. Of those that a mesh axis runs over, the one named last changes fastest.
Arguments:
- queries: bfloat16 [4096, 1024], P('ctx', 'fsdp'), may hold values from -30 to 30
- keys: bfloat16 [4096, 1024], P('ctx', 'fsdp'), may hold values from -10 to 10
- values: bfloat16 [4096, 1024], P('ctx', 'fsdp'), may hold values from -16 to 16
- norm_gain: float32 [1024], P('fsdp'), may hold values from 0.25 to 1.75
- short_filters: float32 [3, 3, 1024], P(None, None, 'fsdp'), may hold values from -3 to 3
- medium_filters: bfloat16 [128, 64], P(None, 'fsdp'), may hold values from -0.5 to 0.5
Outputs:
- mixed: bfloat16 [4096, 1024], P('ctx', 'fsdp')
All inputs are finite; a program needn't handle non-finite values.
Results may differ from a plain program's by a relative error of at most 0.012.
Values may be sent and summed in bfloat16 or wider, within the bound.
A program may use at most 64 MiB of HBM per device.

v0:
```python
import math

import jax
import jax.numpy as jnp
from jax import lax
from jax.sharding import PartitionSpec as P

HEAD_DIM = 128
TAPS = 128
KEY_SPAN = 2


negative_big = -1e30
norm_epsilon = 1e-06


def from_behind(shard, axis, by):
    devices = lax.axis_size(axis)
    pairs = [(i, i + by) for i in range(devices) if 0 <= i + by < devices]
    return lax.ppermute(shard, axis, pairs)


def attend_window(queries_heads, key_rows, value_rows, key_start, query_pos, score_scale, window):
    head_count, rows, head_size = queries_heads.shape
    key_heads = key_rows.reshape(key_rows.shape[0], head_count, head_size).transpose(1, 0, 2)
    value_heads = value_rows.reshape(value_rows.shape[0], head_count, head_size).transpose(1, 0, 2)
    key_pos = key_start + jnp.arange(key_rows.shape[0], dtype=jnp.int32)
    query_block = min(512, rows)

    def one_head(operands):
        query_head, key_head, value_head = operands

        def one_query_block(block_index):
            allowed = (
                (key_pos[None, :] <= query_pos[:, None])
                & (key_pos[None, :] > query_pos[:, None] - window)
                & (key_pos[None, :] >= 0)
            )
            scores = (
                jnp.einsum("qd,kd->qk", query_head, key_head, preferred_element_type=jnp.float32)
                * score_scale
            )
            masked = jnp.where(allowed, scores, negative_big)
            peak = jnp.max(masked, axis=1, keepdims=True)
            exponent = jnp.where(allowed, jnp.exp(masked - peak), 0.0)
            denom = jnp.sum(exponent, axis=1)
            summed = jnp.dot(
                exponent.astype(jnp.bfloat16), value_head, preferred_element_type=jnp.float32
            )
            return summed / denom[:, None]

        pieces = lax.map(one_query_block, jnp.arange(rows // query_block, dtype=jnp.int32))
        return pieces.reshape(rows, head_size)

    return lax.map(one_head, (queries_heads, key_heads, value_heads))


def short_branches(extended, short_filters, out_rows):
    taps_short = short_filters.shape[1]
    channels = extended.shape[1]
    branch = jnp.zeros((3, out_rows, channels), jnp.float32)
    for tap in range(taps_short):
        window = extended[taps_short - 1 - tap : taps_short - 1 - tap + out_rows]
        branch = branch + short_filters[:, tap, None, :] * window[None, :, :]
    return branch


def medium_conv(product_ext, medium_filters, rows):
    ext_rows, channels = product_ext.shape
    taps_long, groups = medium_filters.shape
    block = min(taps_long, rows)
    span = block + taps_long
    base_row = ext_rows - rows
    out_index = jnp.arange(block, dtype=jnp.int32)[:, None]
    ext_index = jnp.arange(span, dtype=jnp.int32)[None, :]
    lag_table = out_index + taps_long - ext_index
    valid = (lag_table >= 0) & (lag_table < taps_long)
    picked = jnp.take(medium_filters, jnp.clip(lag_table, 0, taps_long - 1), axis=0)
    toeplitz = jnp.where(valid[:, :, None], picked, jnp.zeros_like(picked))

    def one_block(block_index):
        start = base_row + block_index * block - taps_long
        piece = lax.dynamic_slice_in_dim(product_ext, start, span, 0).reshape(
            span, groups, channels // groups
        )
        mixed_block = jnp.einsum(
            "teg,egc->tgc", toeplitz, piece, preferred_element_type=jnp.float32
        )
        return mixed_block.reshape(block, channels)

    blocks = lax.map(one_block, jnp.arange(rows // block, dtype=jnp.int32))
    return blocks.reshape(rows, channels)


def per_device(queries, keys, values, norm_gain, short_filters, medium_filters):
    rows, channels = queries.shape
    head_count = channels // HEAD_DIM
    ctx_index = lax.axis_index("ctx")
    window = KEY_SPAN * rows
    query_pos = ctx_index * rows + jnp.arange(rows, dtype=jnp.int32)
    queries_heads = queries.reshape(rows, head_count, HEAD_DIM).transpose(1, 0, 2)
    score_scale = 1.0 / math.sqrt(HEAD_DIM)
    key_list = [keys]
    value_list = [values]
    moving = (keys, values)
    for distance in range(1, KEY_SPAN + 1):
        moving = from_behind((moving[0], moving[1]), "ctx", 1)
        key_list = [moving[0]] + key_list
        value_list = [moving[1]] + value_list
    key_all = jnp.concatenate(key_list, axis=0)
    value_all = jnp.concatenate(value_list, axis=0)
    key_start = (ctx_index - KEY_SPAN) * rows
    heads_out = attend_window(
        queries_heads, key_all, value_all, key_start, query_pos, score_scale, window
    )
    attended = heads_out.transpose(1, 0, 2).reshape(rows, channels).astype(jnp.bfloat16)
    attended_f = attended.astype(jnp.float32)
    local_squares = jnp.sum(attended_f * attended_f, axis=1)
    total_squares = lax.psum(local_squares, "fsdp")
    mean_square = total_squares / (channels * lax.axis_size("fsdp"))
    normed = (
        attended_f * lax.rsqrt(mean_square + norm_epsilon)[:, None] * norm_gain[None, :]
    ).astype(jnp.bfloat16)
    reach = (TAPS + rows) // rows
    margin = short_filters.shape[1] - 1
    earlier = [from_behind(normed, "ctx", 1)]
    normed_ext = jnp.concatenate(earlier + [normed], axis=0).astype(jnp.float32)
    padded = jnp.concatenate([jnp.zeros((margin, channels), jnp.float32), normed_ext], axis=0)
    branch = short_branches(padded, short_filters, (reach + 1) * rows)
    query_branch = branch[0][reach * rows :]
    product_ext = (branch[1] * branch[2]).astype(jnp.bfloat16)
    long_mix = medium_conv(product_ext, medium_filters, rows)
    return (attended_f + query_branch * long_mix).astype(jnp.bfloat16)


def solution(mesh):
    placed = (
        P("ctx", "fsdp"),
        P("ctx", "fsdp"),
        P("ctx", "fsdp"),
        P("fsdp"),
        P(None, None, "fsdp"),
        P(None, "fsdp"),
    )
    return jax.shard_map(
        per_device, mesh=mesh, in_specs=placed, out_specs=P("ctx", "fsdp"), check_vma=False
    )
```

profile of v0, /device:TPU:8, one launch (start us, length us, event | category | flops | bytes accessed | tf_op | source)
XLA Modules:
  0.0 179.3 jit_solution(14497391577238415241)
XLA Ops:
  0.0 1.1 copy.15
  1.1 1.9 %collective-permute-start.2 = (bf16[512,256]{0,1:T(8,128)(2,1)S(1)}, bf16[512,256]{0,1:T(8,128)(2,1)S(1)}, u32[]{:S(2)}, u32[]{:S(2)}) collective-permute-start(bf16[512,256]{0,1:T(8,128)(2,1)S(1)} %copy.15), channel_id=1, source_target_pairs={{0,4},{4,8},{8,12},{12,16},{16,20},{20,24},{24,28},{1,5},{5,9},{9,... | collective-permute-start | bytes 786440 | tf_op jit(solution)/shard_map/ppermute | solution.py:20
  3.0 1.1 copy.13
  4.1 3.6 %collective-permute-start = (bf16[512,256]{0,1:T(8,128)(2,1)S(1)}, bf16[512,256]{0,1:T(8,128)(2,1)S(1)}, u32[]{:S(2)}, u32[]{:S(2)}) collective-permute-start(bf16[512,256]{0,1:T(8,128)(2,1)S(1)} %copy.13), channel_id=1, source_target_pairs={{0,4},{4,8},{8,12},{12,16},{16,20},{20,24},{24,28},{1,5},{5,9},{9,... | collective-permute-start | bytes 786440 | tf_op jit(solution)/shard_map/ppermute | solution.py:20
  7.7 0.1 fusion.36
  7.9 0.2 fusion.42
  8.1 0.7 collective-permute-done.2
  8.8 1.9 %collective-permute-start.3 = (bf16[512,256]{0,1:T(8,128)(2,1)S(1)}, bf16[512,256]{0,1:T(8,128)(2,1)}, u32[]{:S(2)}, u32[]{:S(2)}) collective-permute-start(bf16[512,256]{0,1:T(8,128)(2,1)S(1)} %collective-permute-done.2), channel_id=1, source_target_pairs={{0,4},{4,8},{8,12},{12,16},{16,20},{20,24},{24,28},{1,5},{5,9},{9,... | collective-permute-start | bytes 786440 | tf_op jit(solution)/shard_map/ppermute | solution.py:20
  10.7 0.8 fusion.44
  11.5 0.3 collective-permute-done
  11.8 3.3 %collective-permute-start.1 = (bf16[512,256]{0,1:T(8,128)(2,1)S(1)}, bf16[512,256]{0,1:T(8,128)(2,1)}, u32[]{:S(2)}, u32[]{:S(2)}) collective-permute-start(bf16[512,256]{0,1:T(8,128)(2,1)S(1)} %collective-permute-done), channel_id=1, source_target_pairs={{0,4},{4,8},{8,12},{12,16},{16,20},{20,24},{24,28},{1,5},{5,9},{9,... | collective-permute-start | bytes 786440 | tf_op jit(solution)/shard_map/ppermute | solution.py:20
  15.2 1.1 copy.12
  16.3 0.8 copy.21
  17.1 115.0 %gather_fusion = bf16[32768,16]{1,0:T(8,128)(2,1)} fusion(bf16[128,16]{1,0:T(8,128)(2,1)S(1)} %copy.21, s32[32768]{0:T(1024)S(1)} %broadcast_clamp_fusion), kind=kCustom, calls=%fused_computation | custom fusion | bytes 2228224 | tf_op jit(solution)/shard_map/jit(_take)/gather | solution.py:78
  132.1 7.0 %copy.22 = bf16[128,256,16]{1,0,2:T(8,128)(2,1)S(1)} copy(bf16[128,256,16]{2,1,0:T(8,128)(2,1)} %bitcast.93) | data formatting | bytes 2097152 | tf_op jit(solution)/shard_map/jit(_take)/gather | solution.py:78
  139.2 1.1 pad_maximum_fusion.1
  140.2 1.1 pad_maximum_fusion
  141.3 8.0 %while.32 = (s32[]{:T(128)}, bf16[2,512,128]{2,1,0:T(8,128)(2,1)S(1)}, bf16[2,512,128]{1,2,0:T(8,128)(2,1)S(1)}, bf16[2,1536,128]{1,2,0:T(8,128)(2,1)S(1)}, bf16...) while((s32[]{:T(128)}, bf16[2,512,128]{2,1,0:T(8,128)(2,1)S(1)}, ...), condition=%wide.region_3.4_spmd.clone, body=%wide.region_0.3_spmd.clone.sunk | while | flops 419238400 | bytes 10681441 | solution.py:55
  141.4 1.2 fusion.61
  142.6 1.5 fusion.62
  144.1 1.2 fusion.63
  145.4 1.2 fusion.61
  146.6 1.5 fusion.62
  148.1 1.2 fusion.63
  149.4 0.1 fusion.30
  149.5 9.9 %psum.7 = f32[512]{0:T(512)S(1)} all-reduce(f32[512]{0:T(512)S(1)} %fusion.30), channel_id=1, replica_groups=mesh['ctx'=8,'fsdp'=4] {'fsdp'}, use_global_device_ids=true, to_apply=%region_5.6 | all-reduce | flops 512 | bytes 4096 | tf_op jit(solution)/shard_map/psum | solution.py:119
  159.4 0.1 fusion.33
  159.6 1.9 %collective-permute-start.4 = (bf16[512,256]{1,0:T(8,128)(2,1)S(1)}, bf16[512,256]{1,0:T(8,128)(2,1)S(1)}, u32[]{:S(2)}, u32[]{:S(2)}) collective-permute-start(bf16[512,256]{1,0:T(8,128)(2,1)S(1)} %fusion.33), channel_id=1, source_target_pairs={{0,4},{4,8},{8,12},{12,16},{16,20},{20,24},{24,28},{1,5},{5,9},{9,... | collective-permute-start | bytes 786440 | tf_op jit(solution)/shard_map/ppermute | solution.py:20
  161.5 0.1 select_select_fusion
  161.7 5.6 %collective-permute-done.4 = bf16[512,256]{1,0:T(8,128)(2,1)S(1)} collective-permute-done((bf16[512,256]{1,0:T(8,128)(2,1)S(1)}, bf16[512,256]{1,0:T(8,128)(2,1)S(1)}, u32[]{:S(2)}, u32[]{:S(2)}) %collective-permute-start.4) | collective-permute-done | bytes 262176 | tf_op jit(solution)/shard_map/ppermute | solution.py:20
  167.4 0.1 pad_slice_fusion.1
  167.5 0.5 multiply_add_fusion
  168.1 1.6 copy-done
  169.7 0.1 fusion.31
  169.8 7.6 %while.31 = (s32[]{:T(128)}, f32[4,128,256]{2,1,0:T(8,128)S(1)}, s32[4]{0:T(128)S(1)}, bf16[1024,256]{1,0:T(8,128)(2,1)S(1)}, bf16[128,256,16]{1,0,2:T(8,128)(2,...) while((s32[]{:T(128)}, f32[4,128,256]{2,1,0:T(8,128)S(1)}, s32[4]{0:T(128)S(1)}, ...), condition=%wide.region_7.8_spmd, body=%wide.region_6.7_spmd.sunk | while | flops 16777224 | bytes 2359475 | solution.py:91
  169.8 0.6 dynamic_slice.65
  171.2 0.4 fusion.58
  171.6 0.1 copy.47
  171.7 0.6 dynamic_slice.65
  173.1 0.4 fusion.58
  173.5 0.1 copy.47
  173.6 0.6 dynamic_slice.65
  175.0 0.4 fusion.58
  175.4 0.1 copy.47
  175.5 0.6 dynamic_slice.65
  176.9 0.4 fusion.58
  177.3 0.1 copy.47
  177.4 1.8 %fusion.34 = bf16[512,256]{1,0:T(8,128)(2,1)} fusion(f32[3,1024,256]{2,1,0:T(8,128)} %copy-done, f32[4,128,256]{2,1,0:T(8,128)S(1)} %get-tuple-element.219, bf16[2,512,128]{2,1,0:T(8,128)(2,1)S(1)} %get-tuple-element.218), kind=kLoop, calls=%fused_computation.46 | loop fusion | flops 524288 | bytes 1572864 | tf_op jit(solution)/shard_map/convert_element_type | solution.py:133
  (39 shorter events, 0.8 us)
Async XLA Ops:
  1.1 7.7 %collective-permute-start.2 = (bf16[512,256]{0,1:T(8,128)(2,1)S(1)}, bf16[512,256]{0,1:T(8,128)(2,1)S(1)}, u32[]{:S(2)}, u32[]{:S(2)}) collective-permute-start(bf16[512,256]{0,1:T(8,128)(2,1)S(1)} %copy.15), channel_id=1, source_target_pairs={{0,4},{4,8},{8,12},{12,16},{16,20},{20,24},{24,28},{1,5},{5,9},{9,... | collective-permute-start | bytes 786440 | tf_op jit(solution)/shard_map/ppermute | solution.py:20
  4.1 7.7 %collective-permute-start = (bf16[512,256]{0,1:T(8,128)(2,1)S(1)}, bf16[512,256]{0,1:T(8,128)(2,1)S(1)}, u32[]{:S(2)}, u32[]{:S(2)}) collective-permute-start(bf16[512,256]{0,1:T(8,128)(2,1)S(1)} %copy.13), channel_id=1, source_target_pairs={{0,4},{4,8},{8,12},{12,16},{16,20},{20,24},{24,28},{1,5},{5,9},{9,... | collective-permute-start | bytes 786440 | tf_op jit(solution)/shard_map/ppermute | solution.py:20
  8.8 123.3 %copy-start.3 = (bf16[512,256]{0,1:T(8,128)(2,1)}, bf16[512,256]{0,1:T(8,128)(2,1)S(1)}, u32[]{:S(2)}) copy-start(bf16[512,256]{0,1:T(8,128)(2,1)S(1)} %collective-permute-done.2) | copy-start | bytes 786436
  8.8 130.4 %collective-permute-start.3 = (bf16[512,256]{0,1:T(8,128)(2,1)S(1)}, bf16[512,256]{0,1:T(8,128)(2,1)}, u32[]{:S(2)}, u32[]{:S(2)}) collective-permute-start(bf16[512,256]{0,1:T(8,128)(2,1)S(1)} %collective-permute-done.2), channel_id=1, source_target_pairs={{0,4},{4,8},{8,12},{12,16},{16,20},{20,24},{24,28},{1,5},{5,9},{9,... | collective-permute-start | bytes 786440 | tf_op jit(solution)/shard_map/ppermute | solution.py:20
  11.8 120.3 %copy-start.2 = (bf16[512,256]{0,1:T(8,128)(2,1)}, bf16[512,256]{0,1:T(8,128)(2,1)S(1)}, u32[]{:S(2)}) copy-start(bf16[512,256]{0,1:T(8,128)(2,1)S(1)} %collective-permute-done) | copy-start | bytes 786436
  11.8 128.4 %collective-permute-start.1 = (bf16[512,256]{0,1:T(8,128)(2,1)S(1)}, bf16[512,256]{0,1:T(8,128)(2,1)}, u32[]{:S(2)}, u32[]{:S(2)}) collective-permute-start(bf16[512,256]{0,1:T(8,128)(2,1)S(1)} %collective-permute-done), channel_id=1, source_target_pairs={{0,4},{4,8},{8,12},{12,16},{16,20},{20,24},{24,28},{1,5},{5,9},{9,... | collective-permute-start | bytes 786440 | tf_op jit(solution)/shard_map/ppermute | solution.py:20
  141.3 18.1 %copy-start.4 = (f32[256]{0:T(256)S(1)}, f32[256]{0:T(256)}, u32[]{:S(2)}) copy-start(f32[256]{0:T(256)} %param.13) | copy-start | bytes 3076
  159.6 7.7 %collective-permute-start.4 = (bf16[512,256]{1,0:T(8,128)(2,1)S(1)}, bf16[512,256]{1,0:T(8,128)(2,1)S(1)}, u32[]{:S(2)}, u32[]{:S(2)}) collective-permute-start(bf16[512,256]{1,0:T(8,128)(2,1)S(1)} %fusion.33), channel_id=1, source_target_pairs={{0,4},{4,8},{8,12},{12,16},{16,20},{20,24},{24,28},{1,5},{5,9},{9,... | collective-permute-start | bytes 786440 | tf_op jit(solution)/shard_map/ppermute | solution.py:20
  167.5 2.3 %copy-start.1 = (f32[4,128,256]{2,1,0:T(8,128)S(1)}, f32[4,128,256]{2,1,0:T(8,128)}, u32[]{:S(2)}) copy-start(f32[4,128,256]{2,1,0:T(8,128)} %custom-call.2) | copy-start | bytes 1572868
  168.0 1.7 copy-start
where the time goes:
time: 180 us; the launch traced here: 179 us
  local copies, waits for them, and re-layouts  132 us (73%)
  starting transfers between devices  12.7 us (7%)
  blocking collectives  9.91 us (6%)
  other arithmetic  8.43 us (5%)
  waiting for transfers between devices  6.58 us (4%)
  matrix products  6.38 us (4%)
  loops' own time  2.89 us (2%)
    gather x2, local copies, waits for them, and re-layouts, medium_conv(): jnp.take(medium_filters, jnp.clip(lag_table, 0, taps_long - 1), axis=0)  122 us
    ppermute x5, starting transfers between devices, from_behind(): return lax.ppermute(shard, axis, pairs)  12.7 us
    psum x1, blocking collectives, per_device(): total_squares = lax.psum(local_squares, 'fsdp')  9.91 us
    ppermute x5, waiting for transfers between devices, from_behind(): return lax.ppermute(shard, axis, pairs)  6.58 us
    unnamed x17, local copies, waits for them, and re-layouts  5.81 us
  transfers between devices with their start and end apart: 5, of which 3 were waited for; matrix products, arithmetic and copies ran while one was open for 71% of the time, Pallas kernels for 0%

commit v1 on v0

v1 whole, which is shorter than its diff:
```python
import functools
import math

import jax
import jax.numpy as jnp
from jax import lax
from jax.experimental import pallas as pl
from jax.experimental.pallas import tpu as pltpu
from jax.sharding import PartitionSpec as P

HEAD = 128
LANES = 128
QB = 256
EPS = 1e-06
BIG = -1e30
F32 = jnp.float32
BF16 = jnp.bfloat16
MESH = pl.DeviceIdType.MESH
NT = (((1,), (1,)), ((), ()))

R_Q, R_YK, R_YV, R_O, R_OS, R_HALO, R_X = 0, 1, 2, 3, 4, 5, 6


def scores_of(q_ref, k_ref, h, q0, lo, hi, mode):
    lanes = slice(h * HEAD, (h + 1) * HEAD)
    s = lax.dot_general(
        k_ref[lo:hi, lanes], q_ref[q0 : q0 + QB, lanes], NT, preferred_element_type=F32
    ) * (math.log2(math.e) / math.sqrt(HEAD))
    if mode == "full":
        return s
    key = lax.broadcasted_iota(jnp.int32, (QB, QB), 0)
    query = lax.broadcasted_iota(jnp.int32, (QB, QB), 1)
    at = q0 - lo
    allowed = key <= query if mode == "causal" else key > query
    diag = jnp.where(allowed, s[at : at + QB], BIG)
    parts = ([s[:at]] if at else []) + [diag] + ([s[at + QB :]] if at + QB < hi - lo else [])
    return jnp.concatenate(parts, axis=0) if len(parts) > 1 else diag


def block_attention(q_ref, k_ref, vt_ref, h, q0, mode, m_old):
    rows = k_ref.shape[0]
    lo, hi = {"full": (0, rows), "causal": (0, q0 + QB), "anti": (q0, rows)}[mode]
    s = scores_of(q_ref, k_ref, h, q0, lo, hi, mode)
    m = jnp.max(s, axis=0, keepdims=True)
    if m_old is not None:
        m = jnp.maximum(m, m_old)
    p = jnp.exp2(s - m)
    l = jnp.sum(p, axis=0, keepdims=True)
    o = jnp.dot(
        vt_ref[h * HEAD : (h + 1) * HEAD, lo:hi], p.astype(BF16), preferred_element_type=F32
    )
    return m, l, o


def attend(q_ref, k_ref, vt_ref, h, mode, acc, m_ref, l_ref, first=False):
    for q0 in range(0, q_ref.shape[0], QB):
        cols = slice(q0, q0 + QB)
        ch = slice(h * HEAD, (h + 1) * HEAD)
        row = slice(h, h + 1)
        m_old = None if first else m_ref[row, cols]
        m, l, o = block_attention(q_ref, k_ref, vt_ref, h, q0, mode, m_old)
        if first:
            acc[ch, cols] = o
            l_ref[row, cols] = l
        else:
            a = jnp.exp2(m_old - m)
            acc[ch, cols] = acc[ch, cols] * a + o
            l_ref[row, cols] = l_ref[row, cols] * a + l
        m_ref[row, cols] = m


def kernel(
    n_c, n_f, q, k, v, gain, sf, mf, out,
    vt, xk, xvt, yk, yvt, rq, ot, ost, rot, rost, acc, m_ref, l_ref, att, ssq, rssq,
    wide, cols_ref, toep, nrm, pext, halo, qbr, send, recv,
):
    rows, channels = q.shape
    heads = channels // HEAD
    half = heads // 2
    groups = mf.shape[1]
    size = channels // groups
    blocks = rows // LANES
    c = lax.axis_index("ctx")
    f = lax.axis_index("fsdp")
    core0 = lax.rem(c, 2) == 0
    core1 = lax.rem(c, 2) == 1
    has_prev = c >= 2
    has_next0 = core0 & (c + 2 < n_c)
    has_next1 = core1 & (c + 1 < n_c)

    def copy(src, dst, s, r, dc):
        return pltpu.make_async_remote_copy(
            src_ref=src, dst_ref=dst, send_sem=send.at[s], recv_sem=recv.at[r],
            device_id=(dc, f), device_id_type=MESH,
        )

    def x_parts(h):
        return (
            (xk.at[:, pl.ds(h * HEAD, HEAD)], k.at[:, pl.ds(h * HEAD, HEAD)]),
            (xvt.at[pl.ds(h * HEAD, HEAD)], vt.at[pl.ds(h * HEAD, HEAD)]),
        )

    def x_copy(h, kind, dc, forward):
        dst, own = x_parts(h)[kind]
        s = R_X + 2 * h + kind
        return copy(dst if forward else own, dst, s, s, dc)

    barrier = pltpu.get_barrier_semaphore()
    count = n_f - 1
    for d in range(1, n_f):
        pl.semaphore_signal(
            barrier, inc=1, device_id=(c, lax.rem(f + d, n_f)), device_id_type=MESH
        )
    for d in (1, 2):
        @pl.when(c >= d)
        def _():
            pl.semaphore_signal(barrier, inc=1, device_id=(c - d, f), device_id_type=MESH)

        @pl.when(c + d < n_c)
        def _():
            pl.semaphore_signal(barrier, inc=1, device_id=(c + d, f), device_id_type=MESH)

        count = count + jnp.where(c >= d, 1, 0) + jnp.where(c + d < n_c, 1, 0)
    pl.semaphore_wait(barrier, count)

    cp_q = copy(q, rq, R_Q, R_Q, c - 2)
    cp_yk = copy(k, yk, R_YK, R_YK, c + 1)
    cp_yv = copy(vt, yvt, R_YV, R_YV, c + 1)
    cp_o = copy(ot, rot, R_O, R_O, c + 2)
    cp_os = copy(ost, rost, R_OS, R_OS, c + 2)

    @pl.when(core0 & has_prev)
    def _():
        cp_q.start()

    def each_x(kinds, which, act):
        for h in which:
            for kind in kinds:
                act(h, kind)

    low, high = range(half), range(half, heads)

    @pl.when(has_next1)
    def _():
        each_x((0,), low, lambda h, kind: x_copy(h, kind, c + 1, False).start())
        each_x((0,), high, lambda h, kind: x_copy(h, kind, c + 2, False).start())

    @pl.when(core0)
    def _():
        cp_yk.start()

    for h in range(heads):
        for b in range(blocks):
            piece = v[b * LANES : (b + 1) * LANES, h * HEAD : (h + 1) * HEAD].astype(F32)
            vt[h * HEAD : (h + 1) * HEAD, b * LANES : (b + 1) * LANES] = piece.T.astype(BF16)

    @pl.when(has_next1)
    def _():
        each_x((1,), low, lambda h, kind: x_copy(h, kind, c + 1, False).start())
        each_x((1,), high, lambda h, kind: x_copy(h, kind, c + 2, False).start())

    @pl.when(core0)
    def _():
        cp_yv.start()

    for h in range(heads):
        attend(q, k, vt, h, "causal", acc, m_ref, l_ref, first=True)

    wide[...] = jnp.zeros_like(wide)
    for b in range(3):
        wide[3 * b : 3 * b + 3, :] = sf[b]
    wide[9:10, :] = gain[...]
    for j in range(channels // LANES):
        cols_ref[j * LANES : (j + 1) * LANES, :] = wide[:, j * LANES : (j + 1) * LANES].T
    wide[:, :groups] = mf[...].astype(F32)
    wide[:, LANES : 2 * LANES] = wide[:, :LANES].T
    e = lax.broadcasted_iota(jnp.int32, (LANES, LANES), 0)
    i = lax.broadcasted_iota(jnp.int32, (LANES, LANES), 1)
    for g in range(groups):
        taps = jnp.broadcast_to(wide[g : g + 1, LANES : 2 * LANES], (LANES, LANES))
        ring = pltpu.roll(taps, 0, 1, stride=1, stride_axis=0)
        toep[g, :LANES, :] = jnp.where(i < e, ring, 0.0).astype(BF16)
        toep[g, LANES:, :] = jnp.where(i >= e, ring, 0.0).astype(BF16)

    @pl.when(core1)
    def _():
        copy(k, yk, R_YK, R_YK, c - 1).wait_recv()
        copy(vt, yvt, R_YV, R_YV, c - 1).wait_recv()
        for h in range(heads):
            attend(q, yk, yvt, h, "full", acc, m_ref, l_ref)

    @pl.when(has_next0)
    def _():
        copy(q, rq, R_Q, R_Q, c + 2).wait_recv()
        ost[...] = jnp.zeros_like(ost)
        for h in range(heads):
            for q0 in range(0, rows, QB):
                m, l, o = block_attention(rq, k, vt, h, q0, "anti", None)
                ot[h * HEAD : (h + 1) * HEAD, q0 : q0 + QB] = (o * (1.0 / l)).astype(BF16)
                ost[h : h + 1, q0 : q0 + QB] = m
                ost[heads + h : heads + h + 1, q0 : q0 + QB] = l
        cp_o.start()
        cp_os.start()

    def far(first_heads, later_heads, other, mode):
        for h in first_heads:
            for kind in (0, 1):
                x_copy(h, kind, other, True).wait_recv()
                x_copy(h, kind, other, True).start()
        for h in first_heads:
            attend(q, xk, xvt, h, mode, acc, m_ref, l_ref)
        for h in later_heads:
            for kind in (0, 1):
                x_copy(h, kind, other, True).wait_recv()
            attend(q, xk, xvt, h, mode, acc, m_ref, l_ref)

    @pl.when(core1 & has_prev)
    def _():
        far(high, low, c - 1, "anti")

    @pl.when(core0 & has_prev)
    def _():
        far(low, high, c + 1, "full")
        copy(ot, rot, R_O, R_O, c - 2).wait_recv()
        copy(ost, rost, R_OS, R_OS, c - 2).wait_recv()
        for h in range(heads):
            ch = slice(h * HEAD, (h + 1) * HEAD)
            m_old = m_ref[h : h + 1, :]
            m_far = rost[h : h + 1, :]
            m = jnp.maximum(m_old, m_far)
            a = jnp.exp2(m_old - m)
            b = jnp.exp2(m_far - m) * rost[heads + h : heads + h + 1, :]
            acc[ch, :] = acc[ch, :] * a + rot[ch, :].astype(F32) * b
            l_ref[h : h + 1, :] = l_ref[h : h + 1, :] * a + b

    squares = jnp.zeros((1, rows), F32)
    for h in range(heads):
        ch = slice(h * HEAD, (h + 1) * HEAD)
        done = (acc[ch, :] / l_ref[h : h + 1, :]).astype(BF16)
        att[ch, :] = done
        done = done.astype(F32)
        squares = squares + jnp.sum(done * done, axis=0, keepdims=True)
    ssq[...] = jnp.broadcast_to(squares, ssq.shape)

    base = R_X + 2 * heads

    def ssq_copy(d):
        return pltpu.make_async_remote_copy(
            src_ref=ssq, dst_ref=rssq.at[d - 1], send_sem=send.at[base + d - 1],
            recv_sem=recv.at[base + d - 1],
            device_id=(c, lax.rem(f + d, n_f)), device_id_type=MESH,
        )

    for d in range(1, n_f):
        ssq_copy(d).start()
    total = ssq[0:1, :]
    for d in range(1, n_f):
        ssq_copy(d).wait_recv()
        total = total + rssq[d - 1, 0:1, :]
    scale = lax.rsqrt(total / (channels * n_f) + EPS)
    gain_col = cols_ref[:, 9:10]
    nrm[...] = (att[...].astype(F32) * scale * gain_col).astype(BF16)

    lane = lax.broadcasted_iota(jnp.int32, (channels, LANES), 1)

    def branches(b):
        here = slice(b * LANES, (b + 1) * LANES)
        now = nrm[:, here].astype(F32)
        before = halo[:, LANES:] if b == 0 else nrm[:, (b - 1) * LANES : b * LANES]
        before = before.astype(F32)
        shifted = [now]
        for t in (1, 2):
            shifted.append(
                jnp.where(lane < t, pltpu.roll(before, t, 1), pltpu.roll(now, t, 1))
            )
        total = []
        for n in range(3):
            total.append(
                sum(cols_ref[:, 3 * n + t : 3 * n + t + 1] * shifted[t] for t in range(3))
            )
        qbr[:, here] = total[0]
        return (total[1] * total[2]).astype(BF16)

    halo_src = pext.at[:, pl.ds(blocks * LANES, 2 * LANES)]
    pext[:, blocks * LANES : (blocks + 1) * LANES] = branches(blocks - 1)
    pext[:, (blocks + 1) * LANES :] = nrm[:, (blocks - 1) * LANES :]
    cp_halo = copy(halo_src, halo, R_HALO, R_HALO, c + 1)

    @pl.when(c + 1 < n_c)
    def _():
        cp_halo.start()

    for b in range(blocks - 2, 0, -1):
        pext[:, (b + 1) * LANES : (b + 2) * LANES] = branches(b)

    def mix(which):
        for g in range(groups):
            ch = slice(g * size, (g + 1) * size)
            left = jnp.concatenate(
                [pext[ch, b * LANES : (b + 2) * LANES] for b in which], axis=0
            )
            long = jnp.dot(left, toep[g], preferred_element_type=F32)
            for at, b in enumerate(which):
                here = slice(b * LANES, (b + 1) * LANES)
                acc[ch, here] = (
                    att[ch, here].astype(F32) + qbr[ch, here] * long[at * size : (at + 1) * size]
                )
        for b in which:
            for j in range(channels // LANES):
                piece = acc[j * LANES : (j + 1) * LANES, b * LANES : (b + 1) * LANES]
                out[b * LANES : (b + 1) * LANES, j * LANES : (j + 1) * LANES] = piece.T.astype(BF16)

    mix(list(range(2, blocks)))

    @pl.when(c >= 1)
    def _():
        copy(halo_src, halo, R_HALO, R_HALO, c - 1).wait_recv()

    @pl.when(c == 0)
    def _():
        halo[...] = jnp.zeros_like(halo)

    pext[:, :LANES] = halo[:, :LANES]
    pext[:, LANES : 2 * LANES] = branches(0)
    mix([0, 1])

    @pl.when(core0 & has_prev)
    def _():
        cp_q.wait_send()
        each_x((0, 1), low, lambda h, kind: x_copy(h, kind, c + 1, True).wait_send())

    @pl.when(core1 & has_prev)
    def _():
        each_x((0, 1), high, lambda h, kind: x_copy(h, kind, c - 1, True).wait_send())

    @pl.when(core0)
    def _():
        cp_yk.wait_send()
        cp_yv.wait_send()

    @pl.when(has_next0)
    def _():
        cp_o.wait_send()
        cp_os.wait_send()

    @pl.when(has_next1)
    def _():
        each_x((0, 1), low, lambda h, kind: x_copy(h, kind, c + 1, False).wait_send())
        each_x((0, 1), high, lambda h, kind: x_copy(h, kind, c + 2, False).wait_send())

    for d in range(1, n_f):
        ssq_copy(d).wait_send()

    @pl.when(c + 1 < n_c)
    def _():
        cp_halo.wait_send()


def per_device(n_c, n_f, queries, keys, values, norm_gain, short_filters, medium_filters):
    rows, channels = queries.shape
    heads = channels // HEAD
    groups = medium_filters.shape[1]
    sems = R_X + 2 * heads + n_f
    vmem = pl.BlockSpec(memory_space=pltpu.VMEM)
    long = pltpu.VMEM((rows, channels), BF16)
    turned = pltpu.VMEM((channels, rows), BF16)
    stat = pltpu.VMEM((8, rows), F32)
    return pl.pallas_call(
        functools.partial(kernel, n_c, n_f),
        out_shape=jax.ShapeDtypeStruct((rows, channels), BF16),
        in_specs=[vmem] * 6,
        out_specs=vmem,
        scratch_shapes=[
            turned, long, turned, long, turned,
            long, turned, stat, turned, stat,
            pltpu.VMEM((channels, rows), F32), stat, stat,
            turned, stat, pltpu.VMEM((n_f - 1, 8, rows), F32),
            pltpu.VMEM((LANES, channels), F32),
            pltpu.VMEM((channels, LANES), F32),
            pltpu.VMEM((groups, 2 * LANES, LANES), BF16),
            turned,
            pltpu.VMEM((channels, rows + 2 * LANES), BF16),
            pltpu.VMEM((channels, 2 * LANES), BF16),
            pltpu.VMEM((channels, rows), F32),
            pltpu.SemaphoreType.DMA((sems,)),
            pltpu.SemaphoreType.DMA((sems,)),
        ],
        compiler_params=pltpu.CompilerParams(
            collective_id=0, has_side_effects=True, vmem_limit_bytes=48 * 1024 * 1024
        ),
    )(queries, keys, values, norm_gain.reshape(1, channels), short_filters, medium_filters)


def solution(mesh):
    placed = (
        P("ctx", "fsdp"),
        P("ctx", "fsdp"),
        P("ctx", "fsdp"),
        P("fsdp"),
        P(None, None, "fsdp"),
        P(None, "fsdp"),
    )
    return jax.shard_map(
        functools.partial(per_device, mesh.shape["ctx"], mesh.shape["fsdp"]),
        mesh=mesh, in_specs=placed, out_specs=P("ctx", "fsdp"), check_vma=False,
    )
```

time: 180 us -> 26.1 us (0.15)
  the two profiles are of different devices: /device:TPU:8 before, /device:TPU:9 now
where the time goes in v1:
time: 26.1 us; the launch traced here: 25.9 us
  Pallas kernels  21.4 us (82%)
  local copies, waits for them, and re-layouts  4.39 us (17%)
    pallas_call x1, Pallas kernels, per_device(): pl.pallas_call(functools.partial(kernel, n_c, n_f), out_shape=jax.ShapeDt...  21.4 us
    unnamed x12, local copies, waits for them, and re-layouts  4.39 us

profile of v1, /device:TPU:9, one launch (start us, length us, event | category | flops | bytes accessed | tf_op | source)
XLA Modules:
  0.0 25.9 jit_solution(10481316497667354449)
XLA Ops:
  0.0 0.0 copy-start.3
  0.0 0.0 copy-start.4
  0.0 0.8 %copy.7.mf = bf16[128,16]{1,0:T(8,128)(2,1)S(1)} copy(bf16[128,16]{0,1:T(8,128)(2,1)} %param.11) | data formatting | bytes 8192 | tf_op args[5]
  0.8 0.0 copy-done.3
  0.8 0.0 copy-done.4
  0.8 0.0 copy-start
  0.9 0.9 %copy-done = bf16[512,256]{1,0:T(8,128)(2,1)S(1)} copy-done((bf16[512,256]{1,0:T(8,128)(2,1)S(1)}, bf16[512,256]{1,0:T(8,128)(2,1)}, u32[]{:S(2)}) %copy-start) | copy-done | bytes 262168
  1.8 0.0 copy-start.1
  1.8 0.9 %copy-done.1 = bf16[512,256]{1,0:T(8,128)(2,1)S(1)} copy-done((bf16[512,256]{1,0:T(8,128)(2,1)S(1)}, bf16[512,256]{1,0:T(8,128)(2,1)}, u32[]{:S(2)}) %copy-start.1) | copy-done | bytes 262168
  2.8 0.0 copy-start.2
  2.8 0.9 %copy-done.2 = bf16[512,256]{1,0:T(8,128)(2,1)S(1)} copy-done((bf16[512,256]{1,0:T(8,128)(2,1)S(1)}, bf16[512,256]{1,0:T(8,128)(2,1)}, u32[]{:S(2)}) %copy-start.2) | copy-done | bytes 262168
  3.7 21.4 %shard_map.64 = bf16[512,256]{1,0:T(8,128)(2,1)S(1)} custom-call(bf16[512,256]{1,0:T(8,128)(2,1)S(1)} %copy-done, bf16[512,256]{1,0:T(8,128)(2,1)S(1)} %copy-done.1, bf16[512,256]{1,0:T(8,128)(2,1)S(1)} %copy-done.2, f32[1,256]{1,0:T(1,128)S(1)} %bitcast.1, f32[3,3,256]{2,1,0:T(4,128)S(1)} %copy-done.3, bf16[128,16]{1,0:T(8,128)(2,1)S(1)} %copy.7.mf), custom_call_target="tpu_custom_call" | custom-call | tf_op jit(solution)/shard_map/pallas_call | solution.py:368
  25.2 0.7 %copy.9 = bf16[512,256]{1,0:T(8,128)(2,1)} copy(bf16[512,256]{1,0:T(8,128)(2,1)S(1)} %shard_map.64) | data formatting | bytes 524288
Async XLA Ops:
  0.0 0.8 %copy-start.3 = (f32[3,3,256]{2,1,0:T(4,128)S(1)}, f32[3,3,256]{2,1,0:T(4,128)}, u32[]{:S(2)}) copy-start(f32[3,3,256]{2,1,0:T(4,128)} %sf.1) | copy-start | bytes 27652
  0.0 0.8 %copy-start.4 = (f32[256]{0:T(256)S(1)}, f32[256]{0:T(256)}, u32[]{:S(2)}) copy-start(f32[256]{0:T(256)} %param.9) | copy-start | bytes 3076
  0.8 1.0 %copy-start = (bf16[512,256]{1,0:T(8,128)(2,1)S(1)}, bf16[512,256]{1,0:T(8,128)(2,1)}, u32[]{:S(2)}) copy-start(bf16[512,256]{1,0:T(8,128)(2,1)} %q.1) | copy-start | bytes 786436
  1.8 0.9 %copy-start.1 = (bf16[512,256]{1,0:T(8,128)(2,1)S(1)}, bf16[512,256]{1,0:T(8,128)(2,1)}, u32[]{:S(2)}) copy-start(bf16[512,256]{1,0:T(8,128)(2,1)} %k.1) | copy-start | bytes 786436
  2.8 0.9 %copy-start.2 = (bf16[512,256]{1,0:T(8,128)(2,1)S(1)}, bf16[512,256]{1,0:T(8,128)(2,1)}, u32[]{:S(2)}) copy-start(bf16[512,256]{1,0:T(8,128)(2,1)} %v.1) | copy-start | bytes 786436

commit v2 on v1

v2 whole, which is shorter than its diff:
```python
import functools
import math

import jax
import jax.numpy as jnp
from jax import lax
from jax.experimental import pallas as pl
from jax.experimental.pallas import tpu as pltpu
from jax.sharding import PartitionSpec as P

HEAD = 128
LANES = 128
QB = 256
EPS = 1e-06
BIG = -1e30
F32 = jnp.float32
BF16 = jnp.bfloat16
MESH = pl.DeviceIdType.MESH
NT = (((1,), (1,)), ((), ()))

R_Q, R_YK, R_YV, R_HALO, R_X = 0, 1, 2, 3, 4


def scores_of(q_ref, k_ref, h, q0, lo, hi, mode):
    lanes = slice(h * HEAD, (h + 1) * HEAD)
    s = lax.dot_general(
        k_ref[lo:hi, lanes], q_ref[q0 : q0 + QB, lanes], NT, preferred_element_type=F32
    ) * (math.log2(math.e) / math.sqrt(HEAD))
    if mode == "full":
        return s
    key = lax.broadcasted_iota(jnp.int32, (QB, QB), 0)
    query = lax.broadcasted_iota(jnp.int32, (QB, QB), 1)
    at = q0 - lo
    allowed = key <= query if mode == "causal" else key > query
    diag = jnp.where(allowed, s[at : at + QB], BIG)
    parts = ([s[:at]] if at else []) + [diag] + ([s[at + QB :]] if at + QB < hi - lo else [])
    return jnp.concatenate(parts, axis=0) if len(parts) > 1 else diag


def block_attention(q_ref, k_ref, vt_ref, h, q0, mode, m_old):
    rows = k_ref.shape[0]
    lo, hi = {"full": (0, rows), "causal": (0, q0 + QB), "anti": (q0, rows)}[mode]
    s = scores_of(q_ref, k_ref, h, q0, lo, hi, mode)
    m = jnp.max(s, axis=0, keepdims=True)
    if m_old is not None:
        m = jnp.maximum(m, m_old)
    p = jnp.exp2(s - m)
    l = jnp.sum(p, axis=0, keepdims=True)
    o = jnp.dot(
        vt_ref[h * HEAD : (h + 1) * HEAD, lo:hi], p.astype(BF16), preferred_element_type=F32
    )
    return m, l, o


def attend(q_ref, k_ref, vt_ref, h, q0, mode, acc, m_ref, l_ref, first=False):
    cols = slice(q0, q0 + QB)
    ch = slice(h * HEAD, (h + 1) * HEAD)
    row = slice(h, h + 1)
    m_old = None if first else m_ref[row, cols]
    m, l, o = block_attention(q_ref, k_ref, vt_ref, h, q0, mode, m_old)
    if first:
        acc[ch, cols] = o
        l_ref[row, cols] = l
    else:
        a = jnp.exp2(m_old - m)
        acc[ch, cols] = acc[ch, cols] * a + o
        l_ref[row, cols] = l_ref[row, cols] * a + l
    m_ref[row, cols] = m


def kernel(
    n_c, n_f, q_in, k_in, v_in, gain, sf, mf, out,
    q, k, v, vt, xk, xvt, yk, yvt, rq, ot, ost, rot, rost, acc, m_ref, l_ref, att, ssq, rssq,
    wide, cols_ref, toep, nrm, pext, halo, qbr, send, recv, local,
):
    rows, channels = q.shape
    heads = channels // HEAD
    half = heads // 2
    groups = mf.shape[0]
    size = channels // groups
    blocks = rows // LANES
    n_q = rows // QB
    o_sem = R_X + 2 * heads + n_q * (n_f - 1)
    c = lax.axis_index("ctx")
    f = lax.axis_index("fsdp")
    core0 = lax.rem(c, 2) == 0
    core1 = lax.rem(c, 2) == 1
    has_prev = c >= 2
    has_next0 = core0 & (c + 2 < n_c)
    has_next1 = core1 & (c + 1 < n_c)

    def copy(src, dst, s, r, dc):
        return pltpu.make_async_remote_copy(
            src_ref=src, dst_ref=dst, send_sem=send.at[s], recv_sem=recv.at[r],
            device_id=(dc, f), device_id_type=MESH,
        )

    def x_parts(h):
        return (
            (xk.at[:, pl.ds(h * HEAD, HEAD)], k_in.at[:, pl.ds(h * HEAD, HEAD)]),
            (xvt.at[pl.ds(h * HEAD, HEAD)], vt.at[pl.ds(h * HEAD, HEAD)]),
        )

    def x_copy(h, kind, dc, forward):
        dst, own = x_parts(h)[kind]
        s = R_X + 2 * h + kind
        return copy(dst if forward else own, dst, s, s, dc)

    loads = {}
    for n, (src, dst) in enumerate(((v_in, v), (k_in, k), (q_in, q))):
        for b in range(blocks):
            piece = pl.ds(b * LANES, LANES)
            loads[n, b] = pltpu.make_async_copy(
                src.at[piece], dst.at[piece], local.at[n * blocks + b]
            )
            loads[n, b].start()

    barrier = pltpu.get_barrier_semaphore()
    count = n_f - 1
    for d in range(1, n_f):
        pl.semaphore_signal(
            barrier, inc=1, device_id=(c, lax.rem(f + d, n_f)), device_id_type=MESH
        )
    for d in (1, 2):
        @pl.when(c >= d)
        def _():
            pl.semaphore_signal(barrier, inc=1, device_id=(c - d, f), device_id_type=MESH)

        @pl.when(c + d < n_c)
        def _():
            pl.semaphore_signal(barrier, inc=1, device_id=(c + d, f), device_id_type=MESH)

        count = count + jnp.where(c >= d, 1, 0) + jnp.where(c + d < n_c, 1, 0)
    pl.semaphore_wait(barrier, count)

    cp_q = copy(q_in, rq, R_Q, R_Q, c - 2)
    cp_yk = copy(k_in, yk, R_YK, R_YK, c + 1)
    cp_yv = copy(vt, yvt, R_YV, R_YV, c + 1)

    def o_copies(n, dc):
        piece = pl.ds(n_q * QB - (n + 1) * QB, QB)
        return (
            copy(ot.at[:, piece], rot.at[:, piece], o_sem + 2 * n, o_sem + 2 * n, dc),
            copy(ost.at[:, piece], rost.at[:, piece], o_sem + 2 * n + 1, o_sem + 2 * n + 1, dc),
        )

    @pl.when(core0 & has_prev)
    def _():
        cp_q.start()

    def each_x(kinds, which, act):
        for h in which:
            for kind in kinds:
                act(h, kind)

    low, high = range(half), range(half, heads)

    @pl.when(has_next1)
    def _():
        each_x((0,), low, lambda h, kind: x_copy(h, kind, c + 1, False).start())
        each_x((0,), high, lambda h, kind: x_copy(h, kind, c + 2, False).start())

    @pl.when(core0)
    def _():
        cp_yk.start()

    for b in range(blocks):
        loads[0, b].wait()
        for h in range(heads):
            piece = v[b * LANES : (b + 1) * LANES, h * HEAD : (h + 1) * HEAD].astype(F32)
            vt[h * HEAD : (h + 1) * HEAD, b * LANES : (b + 1) * LANES] = piece.T.astype(BF16)

    @pl.when(has_next1)
    def _():
        each_x((1,), low, lambda h, kind: x_copy(h, kind, c + 1, False).start())
        each_x((1,), high, lambda h, kind: x_copy(h, kind, c + 2, False).start())

    @pl.when(core0)
    def _():
        cp_yv.start()

    for b in range(blocks):
        loads[1, b].wait()
        loads[2, b].wait()
    starts = list(range(0, rows, QB))[::-1]
    for h in range(heads):
        for q0 in starts:
            attend(q, k, vt, h, q0, "causal", acc, m_ref, l_ref, first=True)

    wide[...] = jnp.zeros_like(wide)
    for b in range(3):
        wide[3 * b : 3 * b + 3, :] = sf[b]
    wide[9:10, :] = gain[...]
    for j in range(channels // LANES):
        turned = wide[:, j * LANES : (j + 1) * LANES].T
        for n in range(10):
            cols_ref[n, j * LANES : (j + 1) * LANES, :] = jnp.broadcast_to(
                turned[:, n : n + 1], (LANES, LANES)
            )
    wide[:groups, :LANES] = mf[...].astype(F32)
    e = lax.broadcasted_iota(jnp.int32, (LANES, LANES), 0)
    i = lax.broadcasted_iota(jnp.int32, (LANES, LANES), 1)
    for g in range(groups):
        taps = jnp.broadcast_to(wide[g : g + 1, :LANES], (LANES, LANES))
        ring = pltpu.roll(taps, 0, 1, stride=1, stride_axis=0)
        side = slice(g % 2 * LANES, (g % 2 + 1) * LANES)
        toep[g // 2, :LANES, side] = jnp.where(i < e, ring, 0.0).astype(BF16)
        toep[g // 2, LANES:, side] = jnp.where(i >= e, ring, 0.0).astype(BF16)

    @pl.when(core1)
    def _():
        copy(k_in, yk, R_YK, R_YK, c - 1).wait_recv()
        copy(vt, yvt, R_YV, R_YV, c - 1).wait_recv()
        for h in range(heads):
            for q0 in starts:
                attend(q, yk, yvt, h, q0, "full", acc, m_ref, l_ref)

    @pl.when(has_next0)
    def _():
        copy(q_in, rq, R_Q, R_Q, c + 2).wait_recv()
        ost[...] = jnp.zeros_like(ost)
        for n, q0 in enumerate(starts):
            for h in range(heads):
                m, l, o = block_attention(rq, k, vt, h, q0, "anti", None)
                ot[h * HEAD : (h + 1) * HEAD, q0 : q0 + QB] = (o * (1.0 / l)).astype(BF16)
                ost[h : h + 1, q0 : q0 + QB] = m
                ost[heads + h : heads + h + 1, q0 : q0 + QB] = l
            for cp in o_copies(n, c + 2):
                cp.start()

    def far_first(first_heads, other, mode):
        for h in first_heads:
            for kind in (0, 1):
                x_copy(h, kind, other, True).wait_recv()
                x_copy(h, kind, other, True).start()
        for h in first_heads:
            for q0 in starts:
                attend(q, xk, xvt, h, q0, mode, acc, m_ref, l_ref)

    def far_later(later_heads, other, mode, n):
        for h in later_heads:
            if n == 0:
                for kind in (0, 1):
                    x_copy(h, kind, other, True).wait_recv()
            attend(q, xk, xvt, h, starts[n], mode, acc, m_ref, l_ref)

    @pl.when(core1 & has_prev)
    def _():
        far_first(high, c - 1, "anti")

    @pl.when(core0 & has_prev)
    def _():
        far_first(low, c + 1, "full")

    base = R_X + 2 * heads

    def ssq_copy(n, d):
        piece = pl.ds(starts[n], QB)
        s = base + n * (n_f - 1) + d - 1
        return pltpu.make_async_remote_copy(
            src_ref=ssq.at[:, piece], dst_ref=rssq.at[d - 1, :, piece], send_sem=send.at[s],
            recv_sem=recv.at[s], device_id=(c, lax.rem(f + d, n_f)), device_id_type=MESH,
        )

    for n, q0 in enumerate(starts):
        cols = slice(q0, q0 + QB)

        @pl.when(core1 & has_prev)
        def _():
            far_later(low, c - 1, "anti", n)

        @pl.when(core0 & has_prev)
        def _():
            far_later(high, c + 1, "full", n)
            for cp in o_copies(n, c - 2):
                cp.wait_recv()
            for h in range(heads):
                ch = slice(h * HEAD, (h + 1) * HEAD)
                m_old = m_ref[h : h + 1, cols]
                m_far = rost[h : h + 1, cols]
                m = jnp.maximum(m_old, m_far)
                a = jnp.exp2(m_old - m)
                b = jnp.exp2(m_far - m) * rost[heads + h : heads + h + 1, cols]
                acc[ch, cols] = acc[ch, cols] * a + rot[ch, cols].astype(F32) * b
                l_ref[h : h + 1, cols] = l_ref[h : h + 1, cols] * a + b

        squares = jnp.zeros((1, QB), F32)
        for h in range(heads):
            ch = slice(h * HEAD, (h + 1) * HEAD)
            done = (acc[ch, cols] * (1.0 / l_ref[h : h + 1, cols])).astype(BF16)
            att[ch, cols] = done
            done = done.astype(F32)
            squares = squares + jnp.sum(done * done, axis=0, keepdims=True)
        ssq[:, cols] = jnp.broadcast_to(squares, (8, QB))
        for d in range(1, n_f):
            ssq_copy(n, d).start()

    lane = lax.broadcasted_iota(jnp.int32, (channels, LANES), 1)

    def branches(b):
        here = slice(b * LANES, (b + 1) * LANES)
        now = nrm[:, here].astype(F32)
        before = halo[:, LANES:] if b == 0 else nrm[:, (b - 1) * LANES : b * LANES]
        before = before.astype(F32)
        shifted = [now]
        for t in (1, 2):
            shifted.append(
                jnp.where(lane < t, pltpu.roll(before, t, 1), pltpu.roll(now, t, 1))
            )
        total = []
        for n in range(3):
            total.append(sum(cols_ref[3 * n + t] * shifted[t] for t in range(3)))
        qbr[:, here] = total[0]
        pext[:, (b + 1) * LANES : (b + 2) * LANES] = (total[1] * total[2]).astype(BF16)

    halo_src = pext.at[:, pl.ds(blocks * LANES, 2 * LANES)]
    cp_halo = copy(halo_src, halo, R_HALO, R_HALO, c + 1)
    for n, q0 in enumerate(starts):
        cols = slice(q0, q0 + QB)
        total = ssq[0:1, cols]
        for d in range(1, n_f):
            ssq_copy(n, d).wait_recv()
            total = total + rssq[d - 1, 0:1, cols]
        scale = lax.rsqrt(total / (channels * n_f) + EPS)
        for b in range(q0 // LANES, (q0 + QB) // LANES):
            here = slice(b * LANES, (b + 1) * LANES)
            part = scale[:, b * LANES - q0 : (b + 1) * LANES - q0]
            nrm[:, here] = (att[:, here].astype(F32) * part * cols_ref[9]).astype(BF16)
        ready = range((q0 + QB) // LANES, q0 // LANES, -1)
        for b in ready:
            if b < blocks:
                branches(b)
            if b == blocks - 1:
                pext[:, (blocks + 1) * LANES :] = nrm[:, (blocks - 1) * LANES :]

                @pl.when(c + 1 < n_c)
                def _():
                    cp_halo.start()

    @pl.when(c >= 1)
    def _():
        copy(halo_src, halo, R_HALO, R_HALO, c - 1).wait_recv()

    @pl.when(c == 0)
    def _():
        halo[...] = jnp.zeros_like(halo)

    pext[:, :LANES] = halo[:, :LANES]
    branches(0)
    for pair in range(groups // 2):
        left = [
            pext[g * size : (g + 1) * size, b * LANES : (b + 2) * LANES]
            for g in (2 * pair, 2 * pair + 1)
            for b in range(blocks)
        ]
        long = jnp.dot(
            jnp.concatenate(left, axis=0), toep[pair], preferred_element_type=F32
        )
        for at in range(2 * blocks):
            g, b = 2 * pair + at // blocks, at % blocks
            ch = slice(g * size, (g + 1) * size)
            here = slice(b * LANES, (b + 1) * LANES)
            side = slice(at // blocks * LANES, (at // blocks + 1) * LANES)
            acc[ch, here] = (
                att[ch, here].astype(F32)
                + qbr[ch, here] * long[at * size : (at + 1) * size, side]
            )
    for j in range(channels // LANES):
        for b in range(blocks):
            piece = acc[j * LANES : (j + 1) * LANES, b * LANES : (b + 1) * LANES]
            out[b * LANES : (b + 1) * LANES, j * LANES : (j + 1) * LANES] = piece.T.astype(BF16)

    @pl.when(core0 & has_prev)
    def _():
        cp_q.wait_send()
        each_x((0, 1), low, lambda h, kind: x_copy(h, kind, c + 1, True).wait_send())

    @pl.when(core1 & has_prev)
    def _():
        each_x((0, 1), high, lambda h, kind: x_copy(h, kind, c - 1, True).wait_send())

    @pl.when(core0)
    def _():
        cp_yk.wait_send()
        cp_yv.wait_send()

    @pl.when(has_next0)
    def _():
        for n in range(n_q):
            for cp in o_copies(n, c + 2):
                cp.wait_send()

    @pl.when(has_next1)
    def _():
        each_x((0, 1), low, lambda h, kind: x_copy(h, kind, c + 1, False).wait_send())
        each_x((0, 1), high, lambda h, kind: x_copy(h, kind, c + 2, False).wait_send())

    for n in range(n_q):
        for d in range(1, n_f):
            ssq_copy(n, d).wait_send()

    @pl.when(c + 1 < n_c)
    def _():
        cp_halo.wait_send()


def per_device(n_c, n_f, queries, keys, values, norm_gain, short_filters, medium_filters):
    rows, channels = queries.shape
    heads = channels // HEAD
    groups = medium_filters.shape[1]
    sems = R_X + 2 * heads + (rows // QB) * (n_f + 1)
    hbm = pl.BlockSpec(memory_space=pltpu.HBM)
    vmem = pl.BlockSpec(memory_space=pltpu.VMEM)
    long = pltpu.VMEM((rows, channels), BF16)
    turned = pltpu.VMEM((channels, rows), BF16)
    stat = pltpu.VMEM((8, rows), F32)
    return pl.pallas_call(
        functools.partial(kernel, n_c, n_f),
        out_shape=jax.ShapeDtypeStruct((rows, channels), BF16),
        in_specs=[hbm] * 3 + [vmem] * 3,
        out_specs=vmem,
        scratch_shapes=[
            long, long, long,
            turned, long, turned, long, turned,
            long, turned, stat, turned, stat,
            pltpu.VMEM((channels, rows), F32), stat, stat,
            turned, stat, pltpu.VMEM((n_f - 1, 8, rows), F32),
            pltpu.VMEM((LANES, channels), F32),
            pltpu.VMEM((10, channels, LANES), F32),
            pltpu.VMEM((groups // 2, 2 * LANES, 2 * LANES), BF16),
            turned,
            pltpu.VMEM((channels, rows + 2 * LANES), BF16),
            pltpu.VMEM((channels, 2 * LANES), BF16),
            pltpu.VMEM((channels, rows), F32),
            pltpu.SemaphoreType.DMA((sems,)),
            pltpu.SemaphoreType.DMA((sems,)),
            pltpu.SemaphoreType.DMA((3 * rows // LANES,)),
        ],
        compiler_params=pltpu.CompilerParams(
            collective_id=0, has_side_effects=True, vmem_limit_bytes=56 * 1024 * 1024
        ),
    )(queries, keys, values, norm_gain.reshape(1, channels), short_filters, medium_filters.T)


def solution(mesh):
    placed = (
        P("ctx", "fsdp"),
        P("ctx", "fsdp"),
        P("ctx", "fsdp"),
        P("fsdp"),
        P(None, None, "fsdp"),
        P(None, "fsdp"),
    )
    return jax.shard_map(
        functools.partial(per_device, mesh.shape["ctx"], mesh.shape["fsdp"]),
        mesh=mesh, in_specs=placed, out_specs=P("ctx", "fsdp"), check_vma=False,
    )
```

time: 26.1 us -> 22.2 us (0.85)
  the two profiles are of different devices: /device:TPU:9 before, /device:TPU:8 now
where the time goes in v2:
time: 22.2 us; the launch traced here: 22 us
  Pallas kernels  20.3 us (91%)
  local copies, waits for them, and re-layouts  1.67 us (8%)
    pallas_call x1, Pallas kernels, per_device(): pl.pallas_call(functools.partial(kernel, n_c, n_f), out_shape=jax.ShapeDt...  20.3 us
    unnamed x1, local copies, waits for them, and re-layouts  1.67 us

profile of v2, /device:TPU:8, one launch (start us, length us, event | category | flops | bytes accessed | tf_op | source)
XLA Modules:
  0.0 22.0 jit_solution(6931587893649288247)
XLA Ops:
  0.0 20.3 %shard_map.64 = bf16[512,256]{1,0:T(8,128)(2,1)} custom-call(bf16[512,256]{1,0:T(8,128)(2,1)} %q_in.1, bf16[512,256]{1,0:T(8,128)(2,1)} %k_in.1, bf16[512,256]{1,0:T(8,128)(2,1)} %v_in.1, f32[1,256]{1,0:T(1,128)} %bitcast.3, f32[3,3,256]{2,1,0:T(4,128)} %sf.1, bf16[16,128]{1,0:T(8,128)(2,1)} %bitcast.2), custom_call_target="tpu_custom_call" | custom-call | tf_op jit(solution)/shard_map/pallas_call | solution.py:417
  20.3 1.7 %copy.8 = bf16[512,256]{1,0:T(8,128)(2,1)} copy(bf16[512,256]{1,0:T(8,128)(2,1)} %shard_map.64) | data formatting | bytes 524288

commit v3 on v2

--- a/solution.py
+++ b/solution.py
@@ -37,35 +37,54 @@
     return jnp.concatenate(parts, axis=0) if len(parts) > 1 else diag
 
 
-def block_attention(q_ref, k_ref, vt_ref, h, q0, mode, m_old):
+def span(k_ref, q0, mode):
     rows = k_ref.shape[0]
-    lo, hi = {"full": (0, rows), "causal": (0, q0 + QB), "anti": (q0, rows)}[mode]
-    s = scores_of(q_ref, k_ref, h, q0, lo, hi, mode)
-    m = jnp.max(s, axis=0, keepdims=True)
-    if m_old is not None:
-        m = jnp.maximum(m, m_old)
-    p = jnp.exp2(s - m)
-    l = jnp.sum(p, axis=0, keepdims=True)
-    o = jnp.dot(
-        vt_ref[h * HEAD : (h + 1) * HEAD, lo:hi], p.astype(BF16), preferred_element_type=F32
-    )
-    return m, l, o
+    return {"full": (0, rows), "causal": (0, q0 + QB), "anti": (q0, rows)}[mode]
+
+
+def pipelined(tasks):
+    s = tasks[0][0]()
+    for n, (_, finish) in enumerate(tasks):
+        later = tasks[n + 1][0]() if n + 1 < len(tasks) else None
+        finish(s)
+        s = later
+
+
+def softmax_task(q_ref, k_ref, vt_ref, h, q0, mode, old, write):
+    lo, hi = span(k_ref, q0, mode)
+
+    def finish(s):
+        m = jnp.max(s, axis=0, keepdims=True)
+        m_old = old()
+        if m_old is not None:
+            m = jnp.maximum(m, m_old)
+        p = jnp.exp2(s - m)
+        l = jnp.sum(p, axis=0, keepdims=True)
+        o = jnp.dot(
+            vt_ref[h * HEAD : (h + 1) * HEAD, lo:hi], p.astype(BF16), preferred_element_type=F32
+        )
+        write(m_old, m, l, o)
+
+    return (lambda: scores_of(q_ref, k_ref, h, q0, lo, hi, mode)), finish
 
 
 def attend(q_ref, k_ref, vt_ref, h, q0, mode, acc, m_ref, l_ref, first=False):
     cols = slice(q0, q0 + QB)
     ch = slice(h * HEAD, (h + 1) * HEAD)
     row = slice(h, h + 1)
-    m_old = None if first else m_ref[row, cols]
-    m, l, o = block_attention(q_ref, k_ref, vt_ref, h, q0, mode, m_old)
-    if first:
-        acc[ch, cols] = o
-        l_ref[row, cols] = l
-    else:
-        a = jnp.exp2(m_old - m)
-        acc[ch, cols] = acc[ch, cols] * a + o
-        l_ref[row, cols] = l_ref[row, cols] * a + l
-    m_ref[row, cols] = m
+
+    def write(m_old, m, l, o):
+        if first:
+            acc[ch, cols] = o
+            l_ref[row, cols] = l
+        else:
+            a = jnp.exp2(m_old - m)
+            acc[ch, cols] = acc[ch, cols] * a + o
+            l_ref[row, cols] = l_ref[row, cols] * a + l
+        m_ref[row, cols] = m
+
+    old = (lambda: None) if first else (lambda: m_ref[row, cols])
+    return softmax_task(q_ref, k_ref, vt_ref, h, q0, mode, old, write)
 
 
 def kernel(
@@ -183,9 +202,10 @@
         loads[1, b].wait()
         loads[2, b].wait()
     starts = list(range(0, rows, QB))[::-1]
-    for h in range(heads):
-        for q0 in starts:
-            attend(q, k, vt, h, q0, "causal", acc, m_ref, l_ref, first=True)
+    pipelined([
+        attend(q, k, vt, h, q0, "causal", acc, m_ref, l_ref, first=True)
+        for q0 in starts for h in range(heads)
+    ])
 
     wide[...] = jnp.zeros_like(wide)
     for b in range(3):
@@ -211,38 +231,49 @@
     def _():
         copy(k_in, yk, R_YK, R_YK, c - 1).wait_recv()
         copy(vt, yvt, R_YV, R_YV, c - 1).wait_recv()
-        for h in range(heads):
-            for q0 in starts:
-                attend(q, yk, yvt, h, q0, "full", acc, m_ref, l_ref)
+        pipelined([
+            attend(q, yk, yvt, h, q0, "full", acc, m_ref, l_ref)
+            for q0 in starts for h in range(heads)
+        ])
 
     @pl.when(has_next0)
     def _():
         copy(q_in, rq, R_Q, R_Q, c + 2).wait_recv()
         ost[...] = jnp.zeros_like(ost)
-        for n, q0 in enumerate(starts):
-            for h in range(heads):
-                m, l, o = block_attention(rq, k, vt, h, q0, "anti", None)
-                ot[h * HEAD : (h + 1) * HEAD, q0 : q0 + QB] = (o * (1.0 / l)).astype(BF16)
-                ost[h : h + 1, q0 : q0 + QB] = m
-                ost[heads + h : heads + h + 1, q0 : q0 + QB] = l
-            for cp in o_copies(n, c + 2):
-                cp.start()
+
+        def partial(n, h):
+            cols = slice(starts[n], starts[n] + QB)
+
+            def write(_, m, l, o):
+                ot[h * HEAD : (h + 1) * HEAD, cols] = (o * (1.0 / l)).astype(BF16)
+                ost[h : h + 1, cols] = m
+                ost[heads + h : heads + h + 1, cols] = l
+                if h == heads - 1:
+                    for cp in o_copies(n, c + 2):
+                        cp.start()
+
+            return softmax_task(rq, k, vt, h, starts[n], "anti", lambda: None, write)
+
+        pipelined([partial(n, h) for n in range(n_q) for h in range(heads)])
 
     def far_first(first_heads, other, mode):
         for h in first_heads:
             for kind in (0, 1):
                 x_copy(h, kind, other, True).wait_recv()
                 x_copy(h, kind, other, True).start()
-        for h in first_heads:
-            for q0 in starts:
-                attend(q, xk, xvt, h, q0, mode, acc, m_ref, l_ref)
+        pipelined([
+            attend(q, xk, xvt, h, q0, mode, acc, m_ref, l_ref)
+            for q0 in starts for h in first_heads
+        ])
 
     def far_later(later_heads, other, mode, n):
         for h in later_heads:
             if n == 0:
                 for kind in (0, 1):
                     x_copy(h, kind, other, True).wait_recv()
-            attend(q, xk, xvt, h, starts[n], mode, acc, m_ref, l_ref)
+        pipelined([
+            attend(q, xk, xvt, h, starts[n], mode, acc, m_ref, l_ref) for h in later_heads
+        ])
 
     @pl.when(core1 & has_prev)
     def _():
@@ -365,10 +396,11 @@
                 att[ch, here].astype(F32)
                 + qbr[ch, here] * long[at * size : (at + 1) * size, side]
             )
-    for j in range(channels // LANES):
-        for b in range(blocks):
-            piece = acc[j * LANES : (j + 1) * LANES, b * LANES : (b + 1) * LANES]
-            out[b * LANES : (b + 1) * LANES, j * LANES : (j + 1) * LANES] = piece.T.astype(BF16)
+        if (2 * pair + 2) * size % LANES == 0:
+            j = (2 * pair + 2) * size // LANES - 1
+            for b in range(blocks):
+                piece = acc[j * LANES : (j + 1) * LANES, b * LANES : (b + 1) * LANES]
+                out[b * LANES : (b + 1) * LANES, j * LANES : (j + 1) * LANES] = piece.T.astype(BF16)
 
     @pl.when(core0 & has_prev)
     def _():
@@ -437,7 +469,7 @@
             pltpu.SemaphoreType.DMA((3 * rows // LANES,)),
         ],
         compiler_params=pltpu.CompilerParams(
-            collective_id=0, has_side_effects=True, vmem_limit_bytes=56 * 1024 * 1024
+            collective_id=0, has_side_effects=True, vmem_limit_bytes=54848 * 1024
         ),
     )(queries, keys, values, norm_gain.reshape(1, channels), short_filters, medium_filters.T)
 

time: 22.2 us -> 21.7 us (0.977)
  Pallas kernels: 20.3 us -> 18.6 us
  local copies, waits for them, and re-layouts: 1.67 us -> 2.78 us
    pallas_call x1, Pallas kernels: 20.3 us -> 18.6 us  [per_device(): pl.pallas_call(functools.partial(kernel, n_c, n_f), out_shape=jax.ShapeDt...]
    unnamed x1 -> x7, local copies, waits for them, and re-layouts: 1.67 us -> 2.78 us
where the time goes in v3:
time: 21.7 us; the launch traced here: 21.4 us
  Pallas kernels  18.6 us (86%)
  local copies, waits for them, and re-layouts  2.78 us (13%)
    pallas_call x1, Pallas kernels, per_device(): pl.pallas_call(functools.partial(kernel, n_c, n_f), out_shape=jax.ShapeDt...  18.6 us
    unnamed x7, local copies, waits for them, and re-layouts  2.78 us

profile of v3, /device:TPU:8, one launch (start us, length us, event | category | flops | bytes accessed | tf_op | source)
XLA Modules:
  0.0 21.4 jit_solution(12783958193267925701)
XLA Ops:
  0.0 0.0 copy-start.2
  0.0 0.7 %copy-done.2 = f32[256]{0:T(256)S(1)} copy-done((f32[256]{0:T(256)S(1)}, f32[256]{0:T(256)}, u32[]{:S(2)}) %copy-start.2) | copy-done | bytes 1048
  0.7 0.0 copy-start
  0.7 0.7 %copy-done = f32[3,3,256]{2,1,0:T(4,128)S(1)} copy-done((f32[3,3,256]{2,1,0:T(4,128)S(1)}, f32[3,3,256]{2,1,0:T(4,128)}, u32[]{:S(2)}) %copy-start) | copy-done | bytes 9240
  1.4 0.0 copy-start.1
  1.4 0.7 %copy-done.1 = bf16[128,16]{0,1:T(8,128)(2,1)S(1)} copy-done((bf16[128,16]{0,1:T(8,128)(2,1)S(1)}, bf16[128,16]{0,1:T(8,128)(2,1)}, u32[]{:S(2)}) %copy-start.1) | copy-done | bytes 4120
  2.1 18.6 %shard_map.64 = bf16[512,256]{1,0:T(8,128)(2,1)S(1)} custom-call(bf16[512,256]{1,0:T(8,128)(2,1)} %q_in.1, bf16[512,256]{1,0:T(8,128)(2,1)} %k_in.1, bf16[512,256]{1,0:T(8,128)(2,1)} %v_in.1, f32[1,256]{1,0:T(1,128)S(1)} %bitcast.3, f32[3,3,256]{2,1,0:T(4,128)S(1)} %copy-done, bf16[16,128]{1,0:T(8,128)(2,1)S(1)} %bitcast.2), custom_call_target="tpu_custom_call" | custom-call | tf_op jit(solution)/shard_map/pallas_call | solution.py:449
  20.7 0.7 %copy.8 = bf16[512,256]{1,0:T(8,128)(2,1)} copy(bf16[512,256]{1,0:T(8,128)(2,1)S(1)} %shard_map.64) | data formatting | bytes 524288
Async XLA Ops:
  0.0 0.7 %copy-start.2 = (f32[256]{0:T(256)S(1)}, f32[256]{0:T(256)}, u32[]{:S(2)}) copy-start(f32[256]{0:T(256)} %param.9) | copy-start | bytes 3076
  0.7 0.7 %copy-start = (f32[3,3,256]{2,1,0:T(4,128)S(1)}, f32[3,3,256]{2,1,0:T(4,128)}, u32[]{:S(2)}) copy-start(f32[3,3,256]{2,1,0:T(4,128)} %sf.1) | copy-start | bytes 27652
  1.4 0.7 %copy-start.1 = (bf16[128,16]{0,1:T(8,128)(2,1)S(1)}, bf16[128,16]{0,1:T(8,128)(2,1)}, u32[]{:S(2)}) copy-start(bf16[128,16]{0,1:T(8,128)(2,1)} %param.11) | copy-start | bytes 12292

commit v4 on v3

--- a/solution.py
+++ b/solution.py
@@ -256,32 +256,24 @@
 
         pipelined([partial(n, h) for n in range(n_q) for h in range(heads)])
 
-    def far_first(first_heads, other, mode):
-        for h in first_heads:
-            for kind in (0, 1):
-                x_copy(h, kind, other, True).wait_recv()
-                x_copy(h, kind, other, True).start()
+    def far_first(first_heads, other, mode, n):
+        if n == 0:
+            for h in first_heads:
+                for kind in (0, 1):
+                    x_copy(h, kind, other, True).wait_recv()
+                    x_copy(h, kind, other, True).start()
         pipelined([
-            attend(q, xk, xvt, h, q0, mode, acc, m_ref, l_ref)
-            for q0 in starts for h in first_heads
+            attend(q, xk, xvt, h, starts[n], mode, acc, m_ref, l_ref) for h in first_heads
         ])
 
     def far_later(later_heads, other, mode, n):
-        for h in later_heads:
-            if n == 0:
+        if n == 0:
+            for h in later_heads:
                 for kind in (0, 1):
                     x_copy(h, kind, other, True).wait_recv()
         pipelined([
             attend(q, xk, xvt, h, starts[n], mode, acc, m_ref, l_ref) for h in later_heads
         ])
-
-    @pl.when(core1 & has_prev)
-    def _():
-        far_first(high, c - 1, "anti")
-
-    @pl.when(core0 & has_prev)
-    def _():
-        far_first(low, c + 1, "full")
 
     base = R_X + 2 * heads
 
@@ -292,39 +284,6 @@
             src_ref=ssq.at[:, piece], dst_ref=rssq.at[d - 1, :, piece], send_sem=send.at[s],
             recv_sem=recv.at[s], device_id=(c, lax.rem(f + d, n_f)), device_id_type=MESH,
         )
-
-    for n, q0 in enumerate(starts):
-        cols = slice(q0, q0 + QB)
-
-        @pl.when(core1 & has_prev)
-        def _():
-            far_later(low, c - 1, "anti", n)
-
-        @pl.when(core0 & has_prev)
-        def _():
-            far_later(high, c + 1, "full", n)
-            for cp in o_copies(n, c - 2):
-                cp.wait_recv()
-            for h in range(heads):
-                ch = slice(h * HEAD, (h + 1) * HEAD)
-                m_old = m_ref[h : h + 1, cols]
-                m_far = rost[h : h + 1, cols]
-                m = jnp.maximum(m_old, m_far)
-                a = jnp.exp2(m_old - m)
-                b = jnp.exp2(m_far - m) * rost[heads + h : heads + h + 1, cols]
-                acc[ch, cols] = acc[ch, cols] * a + rot[ch, cols].astype(F32) * b
-                l_ref[h : h + 1, cols] = l_ref[h : h + 1, cols] * a + b
-
-        squares = jnp.zeros((1, QB), F32)
-        for h in range(heads):
-            ch = slice(h * HEAD, (h + 1) * HEAD)
-            done = (acc[ch, cols] * (1.0 / l_ref[h : h + 1, cols])).astype(BF16)
-            att[ch, cols] = done
-            done = done.astype(F32)
-            squares = squares + jnp.sum(done * done, axis=0, keepdims=True)
-        ssq[:, cols] = jnp.broadcast_to(squares, (8, QB))
-        for d in range(1, n_f):
-            ssq_copy(n, d).start()
 
     lane = lax.broadcasted_iota(jnp.int32, (channels, LANES), 1)
 
@@ -346,7 +305,8 @@
 
     halo_src = pext.at[:, pl.ds(blocks * LANES, 2 * LANES)]
     cp_halo = copy(halo_src, halo, R_HALO, R_HALO, c + 1)
-    for n, q0 in enumerate(starts):
+    def normalise(n):
+        q0 = starts[n]
         cols = slice(q0, q0 + QB)
         total = ssq[0:1, cols]
         for d in range(1, n_f):
@@ -367,6 +327,52 @@
                 @pl.when(c + 1 < n_c)
                 def _():
                     cp_halo.start()
+
+    for n, q0 in enumerate(starts):
+        cols = slice(q0, q0 + QB)
+
+        @pl.when(core1 & has_prev)
+        def _():
+            far_first(high, c - 1, "anti", n)
+
+        @pl.when(core0 & has_prev)
+        def _():
+            far_first(low, c + 1, "full", n)
+
+        if n > 0:
+            normalise(n - 1)
+
+        @pl.when(core1 & has_prev)
+        def _():
+            far_later(low, c - 1, "anti", n)
+
+        @pl.when(core0 & has_prev)
+        def _():
+            far_later(high, c + 1, "full", n)
+            for cp in o_copies(n, c - 2):
+                cp.wait_recv()
+            for h in range(heads):
+                ch = slice(h * HEAD, (h + 1) * HEAD)
+                m_old = m_ref[h : h + 1, cols]
+                m_far = rost[h : h + 1, cols]
+                m = jnp.maximum(m_old, m_far)
+                a = jnp.exp2(m_old - m)
+                b = jnp.exp2(m_far - m) * rost[heads + h : heads + h + 1, cols]
+                acc[ch, cols] = acc[ch, cols] * a + rot[ch, cols].astype(F32) * b
+                l_ref[h : h + 1, cols] = l_ref[h : h + 1, cols] * a + b
+
+        squares = jnp.zeros((1, QB), F32)
+        for h in range(heads):
+            ch = slice(h * HEAD, (h + 1) * HEAD)
+            done = (acc[ch, cols] * (1.0 / l_ref[h : h + 1, cols])).astype(BF16)
+            att[ch, cols] = done
+            done = done.astype(F32)
+            squares = squares + jnp.sum(done * done, axis=0, keepdims=True)
+        ssq[:, cols] = jnp.broadcast_to(squares, (8, QB))
+        for d in range(1, n_f):
+            ssq_copy(n, d).start()
+
+    normalise(n_q - 1)
 
     @pl.when(c >= 1)
     def _():
@@ -469,7 +475,7 @@
             pltpu.SemaphoreType.DMA((3 * rows // LANES,)),
         ],
         compiler_params=pltpu.CompilerParams(
-            collective_id=0, has_side_effects=True, vmem_limit_bytes=54848 * 1024
+            collective_id=0, has_side_effects=True, vmem_limit_bytes=56320 * 1024
         ),
     )(queries, keys, values, norm_gain.reshape(1, channels), short_filters, medium_filters.T)
 

time: 21.7 us -> 24.3 us (1.12)
  Pallas kernels: 18.6 us -> 22.4 us
  local copies, waits for them, and re-layouts: 2.78 us -> 1.67 us
    pallas_call x1, Pallas kernels: 18.6 us -> 22.4 us  [per_device(): pl.pallas_call(functools.partial(kernel, n_c, n_f), out_shape=jax.ShapeDt...]
    unnamed x7 -> x1, local copies, waits for them, and re-layouts: 2.78 us -> 1.67 us
where the time goes in v4:
time: 24.3 us; the launch traced here: 24.1 us
  Pallas kernels  22.4 us (92%)
  local copies, waits for them, and re-layouts  1.67 us (7%)
    pallas_call x1, Pallas kernels, per_device(): pl.pallas_call(functools.partial(kernel, n_c, n_f), out_shape=jax.ShapeDt...  22.4 us
    unnamed x1, local copies, waits for them, and re-layouts  1.67 us

profile of v4, /device:TPU:8, one launch (start us, length us, event | category | flops | bytes accessed | tf_op | source)
XLA Modules:
  0.0 24.1 jit_solution(17231641100872025671)
XLA Ops:
  0.0 22.4 %shard_map.64 = bf16[512,256]{1,0:T(8,128)(2,1)} custom-call(bf16[512,256]{1,0:T(8,128)(2,1)} %q_in.1, bf16[512,256]{1,0:T(8,128)(2,1)} %k_in.1, bf16[512,256]{1,0:T(8,128)(2,1)} %v_in.1, f32[1,256]{1,0:T(1,128)} %bitcast.3, f32[3,3,256]{2,1,0:T(4,128)} %sf.1, bf16[16,128]{1,0:T(8,128)(2,1)} %bitcast.2), custom_call_target="tpu_custom_call" | custom-call | tf_op jit(solution)/shard_map/pallas_call | solution.py:455
  22.4 1.7 %copy.8 = bf16[512,256]{1,0:T(8,128)(2,1)} copy(bf16[512,256]{1,0:T(8,128)(2,1)} %shard_map.64) | data formatting | bytes 524288

commit v5 on v3

--- a/solution.py
+++ b/solution.py
@@ -469,7 +469,7 @@
             pltpu.SemaphoreType.DMA((3 * rows // LANES,)),
         ],
         compiler_params=pltpu.CompilerParams(
-            collective_id=0, has_side_effects=True, vmem_limit_bytes=54848 * 1024
+            collective_id=0, has_side_effects=True, vmem_limit_bytes=55600 * 1024
         ),
     )(queries, keys, values, norm_gain.reshape(1, channels), short_filters, medium_filters.T)
 

time: 21.7 us -> 21.9 us (level)
  Pallas kernels: 18.6 us -> 20 us
  local copies, waits for them, and re-layouts: 2.78 us -> 1.67 us
    pallas_call x1, Pallas kernels: 18.6 us -> 20 us  [per_device(): pl.pallas_call(functools.partial(kernel, n_c, n_f), out_shape=jax.ShapeDt...]
    unnamed x7 -> x1, local copies, waits for them, and re-layouts: 2.78 us -> 1.67 us
where the time goes in v5:
time: 21.9 us; the launch traced here: 21.7 us
  Pallas kernels  20 us (91%)
  local copies, waits for them, and re-layouts  1.67 us (8%)
    pallas_call x1, Pallas kernels, per_device(): pl.pallas_call(functools.partial(kernel, n_c, n_f), out_shape=jax.ShapeDt...  20 us
    unnamed x1, local copies, waits for them, and re-layouts  1.67 us

profile of v5, /device:TPU:8, one launch (start us, length us, event | category | flops | bytes accessed | tf_op | source)
XLA Modules:
  0.0 21.7 jit_solution(10567871885734138164)
XLA Ops:
  0.0 20.0 %shard_map.64 = bf16[512,256]{1,0:T(8,128)(2,1)} custom-call(bf16[512,256]{1,0:T(8,128)(2,1)} %q_in.1, bf16[512,256]{1,0:T(8,128)(2,1)} %k_in.1, bf16[512,256]{1,0:T(8,128)(2,1)} %v_in.1, f32[1,256]{1,0:T(1,128)} %bitcast.3, f32[3,3,256]{2,1,0:T(4,128)} %sf.1, bf16[16,128]{1,0:T(8,128)(2,1)} %bitcast.2), custom_call_target="tpu_custom_call" | custom-call | tf_op jit(solution)/shard_map/pallas_call | solution.py:449
  20.0 1.7 %copy.8 = bf16[512,256]{1,0:T(8,128)(2,1)} copy(bf16[512,256]{1,0:T(8,128)(2,1)} %shard_map.64) | data formatting | bytes 524288

commit v6 on v5

--- a/solution.py
+++ b/solution.py
@@ -88,9 +88,9 @@
 
 
 def kernel(
-    n_c, n_f, q_in, k_in, v_in, gain, sf, mf, out,
-    q, k, v, vt, xk, xvt, yk, yvt, rq, ot, ost, rot, rost, acc, m_ref, l_ref, att, ssq, rssq,
-    wide, cols_ref, toep, nrm, pext, halo, qbr, send, recv, local,
+    n_c, n_f, q, k, v, gain, sf, mf, out,
+    vt, xk, xvt, yk, yvt, rq, ot, ost, rot, rost, acc, m_ref, l_ref, att, ssq, rssq,
+    wide, cols_ref, toep, nrm, pext, halo, qbr, send, recv,
 ):
     rows, channels = q.shape
     heads = channels // HEAD
@@ -116,7 +116,7 @@
 
     def x_parts(h):
         return (
-            (xk.at[:, pl.ds(h * HEAD, HEAD)], k_in.at[:, pl.ds(h * HEAD, HEAD)]),
+            (xk.at[:, pl.ds(h * HEAD, HEAD)], k.at[:, pl.ds(h * HEAD, HEAD)]),
             (xvt.at[pl.ds(h * HEAD, HEAD)], vt.at[pl.ds(h * HEAD, HEAD)]),
         )
 
@@ -124,15 +124,6 @@
         dst, own = x_parts(h)[kind]
         s = R_X + 2 * h + kind
         return copy(dst if forward else own, dst, s, s, dc)
-
-    loads = {}
-    for n, (src, dst) in enumerate(((v_in, v), (k_in, k), (q_in, q))):
-        for b in range(blocks):
-            piece = pl.ds(b * LANES, LANES)
-            loads[n, b] = pltpu.make_async_copy(
-                src.at[piece], dst.at[piece], local.at[n * blocks + b]
-            )
-            loads[n, b].start()
 
     barrier = pltpu.get_barrier_semaphore()
     count = n_f - 1
@@ -152,8 +143,8 @@
         count = count + jnp.where(c >= d, 1, 0) + jnp.where(c + d < n_c, 1, 0)
     pl.semaphore_wait(barrier, count)
 
-    cp_q = copy(q_in, rq, R_Q, R_Q, c - 2)
-    cp_yk = copy(k_in, yk, R_YK, R_YK, c + 1)
+    cp_q = copy(q, rq, R_Q, R_Q, c - 2)
+    cp_yk = copy(k, yk, R_YK, R_YK, c + 1)
     cp_yv = copy(vt, yvt, R_YV, R_YV, c + 1)
 
     def o_copies(n, dc):
@@ -184,7 +175,6 @@
         cp_yk.start()
 
     for b in range(blocks):
-        loads[0, b].wait()
         for h in range(heads):
             piece = v[b * LANES : (b + 1) * LANES, h * HEAD : (h + 1) * HEAD].astype(F32)
             vt[h * HEAD : (h + 1) * HEAD, b * LANES : (b + 1) * LANES] = piece.T.astype(BF16)
@@ -198,9 +188,6 @@
     def _():
         cp_yv.start()
 
-    for b in range(blocks):
-        loads[1, b].wait()
-        loads[2, b].wait()
     starts = list(range(0, rows, QB))[::-1]
     pipelined([
         attend(q, k, vt, h, q0, "causal", acc, m_ref, l_ref, first=True)
@@ -229,7 +216,7 @@
 
     @pl.when(core1)
     def _():
-        copy(k_in, yk, R_YK, R_YK, c - 1).wait_recv()
+        copy(k, yk, R_YK, R_YK, c - 1).wait_recv()
         copy(vt, yvt, R_YV, R_YV, c - 1).wait_recv()
         pipelined([
             attend(q, yk, yvt, h, q0, "full", acc, m_ref, l_ref)
@@ -238,7 +225,7 @@
 
     @pl.when(has_next0)
     def _():
-        copy(q_in, rq, R_Q, R_Q, c + 2).wait_recv()
+        copy(q, rq, R_Q, R_Q, c + 2).wait_recv()
         ost[...] = jnp.zeros_like(ost)
 
         def partial(n, h):
@@ -441,7 +428,6 @@
     heads = channels // HEAD
     groups = medium_filters.shape[1]
     sems = R_X + 2 * heads + (rows // QB) * (n_f + 1)
-    hbm = pl.BlockSpec(memory_space=pltpu.HBM)
     vmem = pl.BlockSpec(memory_space=pltpu.VMEM)
     long = pltpu.VMEM((rows, channels), BF16)
     turned = pltpu.VMEM((channels, rows), BF16)
@@ -449,10 +435,9 @@
     return pl.pallas_call(
         functools.partial(kernel, n_c, n_f),
         out_shape=jax.ShapeDtypeStruct((rows, channels), BF16),
-        in_specs=[hbm] * 3 + [vmem] * 3,
+        in_specs=[vmem] * 6,
         out_specs=vmem,
         scratch_shapes=[
-            long, long, long,
             turned, long, turned, long, turned,
             long, turned, stat, turned, stat,
             pltpu.VMEM((channels, rows), F32), stat, stat,
@@ -466,10 +451,9 @@
             pltpu.VMEM((channels, rows), F32),
             pltpu.SemaphoreType.DMA((sems,)),
             pltpu.SemaphoreType.DMA((sems,)),
-            pltpu.SemaphoreType.DMA((3 * rows // LANES,)),
         ],
         compiler_params=pltpu.CompilerParams(
-            collective_id=0, has_side_effects=True, vmem_limit_bytes=55600 * 1024
+            collective_id=0, has_side_effects=True, vmem_limit_bytes=32 * 1024 * 1024
         ),
     )(queries, keys, values, norm_gain.reshape(1, channels), short_filters, medium_filters.T)
 

time: 21.9 us -> 24.2 us (1.11)
  local copies, waits for them, and re-layouts: 1.67 us -> 5.62 us
  Pallas kernels: 20 us -> 18.3 us
    unnamed x1 -> x13, local copies, waits for them, and re-layouts: 1.67 us -> 5.62 us
    pallas_call x1, Pallas kernels: 20 us -> 18.3 us  [per_device(): pl.pallas_call(functools.partial(kernel, n_c, n_f), out_shape=jax.ShapeDt...]
where the time goes in v6:
time: 24.2 us; the launch traced here: 23.9 us
  Pallas kernels  18.3 us (76%)
  local copies, waits for them, and re-layouts  5.62 us (23%)
    pallas_call x1, Pallas kernels, per_device(): pl.pallas_call(functools.partial(kernel, n_c, n_f), out_shape=jax.ShapeDt...  18.3 us
    unnamed x13, local copies, waits for them, and re-layouts  5.62 us

profile of v6, /device:TPU:8, one launch (start us, length us, event | category | flops | bytes accessed | tf_op | source)
XLA Modules:
  0.0 23.9 jit_solution(6976314114311194283)
XLA Ops:
  0.0 0.0 copy-start.5
  0.0 0.7 %copy-done.5 = f32[256]{0:T(256)S(1)} copy-done((f32[256]{0:T(256)S(1)}, f32[256]{0:T(256)}, u32[]{:S(2)}) %copy-start.5) | copy-done | bytes 1048
  0.7 0.0 copy-start
  0.7 0.9 %copy-done = bf16[512,256]{1,0:T(8,128)(2,1)S(1)} copy-done((bf16[512,256]{1,0:T(8,128)(2,1)S(1)}, bf16[512,256]{1,0:T(8,128)(2,1)}, u32[]{:S(2)}) %copy-start) | copy-done | bytes 262168
  1.6 0.0 copy-start.1
  1.6 0.9 %copy-done.1 = bf16[512,256]{1,0:T(8,128)(2,1)S(1)} copy-done((bf16[512,256]{1,0:T(8,128)(2,1)S(1)}, bf16[512,256]{1,0:T(8,128)(2,1)}, u32[]{:S(2)}) %copy-start.1) | copy-done | bytes 262168
  2.6 0.0 copy-start.2
  2.6 0.9 %copy-done.2 = bf16[512,256]{1,0:T(8,128)(2,1)S(1)} copy-done((bf16[512,256]{1,0:T(8,128)(2,1)S(1)}, bf16[512,256]{1,0:T(8,128)(2,1)}, u32[]{:S(2)}) %copy-start.2) | copy-done | bytes 262168
  3.5 0.0 copy-start.3
  3.5 0.7 %copy-done.3 = f32[3,3,256]{2,1,0:T(4,128)S(1)} copy-done((f32[3,3,256]{2,1,0:T(4,128)S(1)}, f32[3,3,256]{2,1,0:T(4,128)}, u32[]{:S(2)}) %copy-start.3) | copy-done | bytes 9240
  4.2 0.0 copy-start.4
  4.2 0.7 %copy-done.4 = bf16[128,16]{0,1:T(8,128)(2,1)S(1)} copy-done((bf16[128,16]{0,1:T(8,128)(2,1)S(1)}, bf16[128,16]{0,1:T(8,128)(2,1)}, u32[]{:S(2)}) %copy-start.4) | copy-done | bytes 4120
  4.9 18.3 %shard_map.64 = bf16[512,256]{1,0:T(8,128)(2,1)S(1)} custom-call(bf16[512,256]{1,0:T(8,128)(2,1)S(1)} %copy-done, bf16[512,256]{1,0:T(8,128)(2,1)S(1)} %copy-done.1, bf16[512,256]{1,0:T(8,128)(2,1)S(1)} %copy-done.2, f32[1,256]{1,0:T(1,128)S(1)} %bitcast.3, f32[3,3,256]{2,1,0:T(4,128)S(1)} %copy-done.3, bf16[16,128]{1,0:T(8,128)(2,1)S(1)} %bitcast.2), custom_call_target="tpu_custom_call" | custom-call | tf_op jit(solution)/shard_map/pallas_call | solution.py:435
  23.2 0.7 %copy.8 = bf16[512,256]{1,0:T(8,128)(2,1)} copy(bf16[512,256]{1,0:T(8,128)(2,1)S(1)} %shard_map.64) | data formatting | bytes 524288
Async XLA Ops:
  0.0 0.7 %copy-start.5 = (f32[256]{0:T(256)S(1)}, f32[256]{0:T(256)}, u32[]{:S(2)}) copy-start(f32[256]{0:T(256)} %param.9) | copy-start | bytes 3076
  0.7 0.9 %copy-start = (bf16[512,256]{1,0:T(8,128)(2,1)S(1)}, bf16[512,256]{1,0:T(8,128)(2,1)}, u32[]{:S(2)}) copy-start(bf16[512,256]{1,0:T(8,128)(2,1)} %q.1) | copy-start | bytes 786436
  1.6 0.9 %copy-start.1 = (bf16[512,256]{1,0:T(8,128)(2,1)S(1)}, bf16[512,256]{1,0:T(8,128)(2,1)}, u32[]{:S(2)}) copy-start(bf16[512,256]{1,0:T(8,128)(2,1)} %k.1) | copy-start | bytes 786436
  2.6 0.9 %copy-start.2 = (bf16[512,256]{1,0:T(8,128)(2,1)S(1)}, bf16[512,256]{1,0:T(8,128)(2,1)}, u32[]{:S(2)}) copy-start(bf16[512,256]{1,0:T(8,128)(2,1)} %v.1) | copy-start | bytes 786436
  3.5 0.7 %copy-start.3 = (f32[3,3,256]{2,1,0:T(4,128)S(1)}, f32[3,3,256]{2,1,0:T(4,128)}, u32[]{:S(2)}) copy-start(f32[3,3,256]{2,1,0:T(4,128)} %sf.1) | copy-start | bytes 27652
  4.2 0.7 %copy-start.4 = (bf16[128,16]{0,1:T(8,128)(2,1)S(1)}, bf16[128,16]{0,1:T(8,128)(2,1)}, u32[]{:S(2)}) copy-start(bf16[128,16]{0,1:T(8,128)(2,1)} %param.11) | copy-start | bytes 12292
